TPU v7x, 32 devices: a whole 2x2x4 slice. The times are simulated.
32 devices in a mesh: groups: 2 (over x), owner: 16 (over z, y, core).
Axes of the slice: x: 2, y: 2, z: 4, core: 2. Of those that a mesh axis runs over, the one named last changes fastest.
Arguments:
- embeddings: bfloat16 [65536, 256], P(('groups', 'owner')), parts along dimension 0, may hold values from -6 to 6
- code_one: int32 [65536], P(('groups', 'owner')), parts along dimension 0, may hold values from 0 to 127, as said below
- code_two: int32 [65536], P(('groups', 'owner')), parts along dimension 0, may hold values from 0 to 1023
- parent_slot: int32 [256], P('groups'), parts along dimension 0, may hold values from 0 to 127, as said below
- centers_one: float32 [256, 256], P('groups'), parts along dimension 0, may hold values from -6 to 6
- centers_two: bfloat16 [256, 1024, 256], P(('groups', 'owner')), parts along dimension 0, may hold values from -6 to 6
Outputs:
- new_one: float32 [256, 256], P('groups'), parts along dimension 0
- new_two: bfloat16 [256, 1024, 256], P(('groups', 'owner')), parts along dimension 0
- residual_two: bfloat16 [65536, 256], P(('groups', 'owner')), parts along dimension 0
There are 2 independent parts, one for each index of `groups`. A program takes and returns all parts, laid end to end along the dimension named above; each array names one. Nothing has to cross between parts.
Inputs may be any that keep to these rules, and one draw needn't show every extreme that they name: A permutation: the codebook of level-1 codeword p is row parent_slot[p] of centers_two. `code_one`: count the codewords p with parent_slot[p] // 8 = o as those of owner o. The 2048 entities of one owner index have at most 256 level-1 codes of any one owner; one owner receives exactly this many from every owner index.
All inputs are finite; a program needn't handle non-finite values.
Results may differ from a plain program's by a relative error of at most 0.0004.
Values may be sent and summed in bfloat16 or wider, within the bound.
A program may use at most 128 MiB of HBM per device.

v0:
```python
import jax
import jax.numpy as jnp
from jax import lax
from jax.sharding import PartitionSpec as P

prior_one = 16.0
prior_two = 1.0


def lookup_slot(codes, parent_slot):
    parent_ids = jnp.arange(parent_slot.shape[0], dtype=jnp.int32)
    matched = codes[None, :] == parent_ids[:, None]
    return jnp.sum(jnp.where(matched, parent_slot[:, None], 0), 0)


def shards(embeddings, code_one, code_two, parent_slot, centers_one, centers_two):
    row_count, feature_width = embeddings.shape
    owner_count = lax.axis_size("owner")
    parent_count = centers_one.shape[0]
    local_books = centers_two.shape[0]
    codewords = centers_two.shape[1]
    capacity = 2 * row_count // owner_count
    own_index = lax.axis_index("owner")
    parent_ids = jnp.arange(parent_count, dtype=jnp.int32)
    select = (code_one[None, :] == parent_ids[:, None]).astype(jnp.bfloat16)
    partial_value = jnp.dot(select, embeddings, preferred_element_type=jnp.float32)
    tallies = jnp.sum(select, axis=1, dtype=jnp.float32)
    slot_of = lookup_slot(code_one, parent_slot)
    target = slot_of // local_books
    owner_hits = (target[:, None] == jnp.arange(owner_count, dtype=jnp.int32)[None, :]).astype(
        jnp.int32
    )
    arrival_rank = jnp.sum(jnp.cumsum(owner_hits, 0) * owner_hits, 1) - 1
    position = target * capacity + arrival_rank
    code_word = code_one * codewords + code_two
    code_buffer = jnp.full((owner_count * capacity,), -1, jnp.int32).at[position].set(code_word)
    code_buffer = code_buffer.reshape(owner_count, capacity)
    summed, counted = lax.psum((partial_value, tallies), "owner")
    new_one = (summed + prior_one * centers_one) / (counted[:, None] + prior_one)
    residual = embeddings.astype(jnp.float32) - jnp.take(new_one, code_one, axis=0)
    row_buffer = (
        jnp.zeros((owner_count * capacity, feature_width), jnp.float32).at[position].set(residual)
    )
    arrived, arrived_codes = (
        lax.all_to_all(
            row_buffer.reshape(owner_count, capacity, feature_width),
            "owner",
            split_axis=0,
            concat_axis=0,
            tiled=True,
        ),
        lax.all_to_all(code_buffer, "owner", split_axis=0, concat_axis=0, tiled=True),
    )
    flat_codes = arrived_codes.reshape(owner_count * capacity)
    live = flat_codes >= 0
    parent_in = jnp.where(live, flat_codes // codewords, 0)
    resid_in = arrived.reshape(owner_count * capacity, feature_width)
    word_in = jnp.where(live, flat_codes % codewords, 0)
    local_in = lookup_slot(parent_in, parent_slot) - own_index * local_books
    dump_cell = local_books * codewords
    segment = jnp.where(live, local_in * codewords + word_in, dump_cell)
    sums_two = jax.ops.segment_sum(resid_in, segment, num_segments=dump_cell + 1)[:dump_cell]
    counts_two = jax.ops.segment_sum(live.astype(jnp.float32), segment, num_segments=dump_cell + 1)[
        :dump_cell
    ]
    refined = (
        sums_two.reshape(local_books, codewords, feature_width)
        + prior_two * centers_two.astype(jnp.float32)
    ) / (counts_two.reshape(local_books, codewords, 1) + prior_two)
    flat_refined = refined.reshape(dump_cell, feature_width)
    outgoing = (resid_in - jnp.take(flat_refined, jnp.where(live, segment, 0), axis=0)).astype(
        jnp.bfloat16
    )
    outgoing = jnp.where(live[:, None], outgoing, jnp.zeros((), jnp.bfloat16))
    returned = lax.all_to_all(
        outgoing.reshape(owner_count, capacity, feature_width),
        "owner",
        split_axis=0,
        concat_axis=0,
        tiled=True,
    )
    residual_two = returned.reshape(owner_count * capacity, feature_width)[position]
    return (new_one, refined.astype(jnp.bfloat16), residual_two)


def solution(mesh):
    placed = (
        P(("groups", "owner"), None),
        P(("groups", "owner")),
        P(("groups", "owner")),
        P("groups"),
        P("groups", None),
        P(("groups", "owner"), None, None),
    )
    return jax.shard_map(
        shards,
        mesh=mesh,
        in_specs=placed,
        out_specs=(
            P("groups", None),
            P(("groups", "owner"), None, None),
            P(("groups", "owner"), None),
        ),
        check_vma=False,
    )
```

profile of v0, /device:TPU:13, one launch (start us, length us, event | category | flops | bytes accessed | tf_op | source)
XLA Modules:
  0.0 374.9 jit_solution(12274198809396504691)
XLA Ops:
  7.2 1.0 select_reduce_fusion.1
  8.2 0.7 fusion.36
  8.9 4.5 %reduce-window.6 = s32[16,16,128]{2,1,0:T(8,128)S(1)} reduce-window(s32[16,16,128]{2,1,0:T(8,128)S(1)} %fusion.15, s32[]{:T(128)} %constant.88.clone.1), window={size=1x1x128 pad=0_0x0_0x127_0}, to_apply=%region_4.5 | reduce-window | flops 4161536 | bytes 262148 | tf_op jit(solution)/shard_map/reduce-window
  14.3 8.6 %scatter_custom_fusion = s32[4096]{0:T(1024)} fusion(s32[2048]{0:T(1024)S(1)} %bitcast.67, s32[2048]{0:T(1024)S(1)} %get-tuple-element.10, s32[]{:T(128)} %constant.87.clone.1), kind=kCustom, calls=%fused_computation.91 | custom fusion | bytes 16388 | tf_op jit(solution)/shard_map/scatter | solution.py:36
  22.9 6.6 %all-to-all-start = ((s32[16,1,256]{2,1,0:T(1,128)}), s32[16,1,256]{2,1,0:T(1,128)S(1)}, u32[]{:S(2)}, u32[]{:S(2)}) async-start(s32[16,1,256]{2,1,0:T(1,128)} %bitcast.5), calls=%async_computation | async-start | bytes 32768 | tf_op jit(solution)/shard_map/all_to_all | solution.py:52
  29.5 2.2 fusion.10
  31.7 0.9 convert_reduce_fusion
  32.6 0.7 compare_and_fusion.1
  33.3 21.7 %psum.15 = f32[128]{0:T(128)S(1)} all-reduce(f32[128]{0:T(128)S(1)} %convert_reduce_fusion), channel_id=1, replica_groups=mesh['groups'=2,'owner'=16] {'owner'}, use_global_device_ids=true, to_apply=%region_2.3 | all-reduce | flops 128 | bytes 1024 | tf_op jit(solution)/shard_map/psum | solution.py:38
  55.1 65.7 %all-reduce.2.cloned.1.call-done = f32[128,256]{1,0:T(8,128)} async-done(((f32[128,256]{1,0:T(8,128)}), f32[128,256]{1,0:T(8,128)}) %all-reduce.2.cloned.1.call-update) | async-done | bytes 131088 | tf_op jit(solution)/shard_map/psum | solution.py:38
  120.8 1.1 add_divide_fusion.1
  121.8 19.2 %scatter_custom_fusion.1 = f32[4096,256]{1,0:T(8,128)} fusion(s32[2048]{0:T(1024)S(1)} %bitcast.68, bf16[2048,256]{1,0:T(8,128)(2,1)} %param.6, f32[]{:T(128)} %constant.86.clone.1, f32[]{:T(128)} %constant.102.clone.1, pred[2048]{0:T(1024)(128)(4,1)S(1)} %compare_and_fusion.1, f32[128,256]{1,0:T(8,128)S(1)} %add_divide_fusion.1, s32[2048]{0:T(1024)S(1)} %get-tuple-element.9), kind=kCustom, calls=%fused_computation.12 | custom fusion | flops 1572864 | bytes 5384200 | tf_op jit(solution)/shard_map/scatter | solution.py:42
  141.1 8.4 %all-to-all-start.1 = ((f32[16,256,256]{2,1,0:T(8,128)}), f32[16,256,256]{2,1,0:T(8,128)}, u32[]{:S(2)}, u32[]{:S(2)}) async-start(f32[16,256,256]{2,1,0:T(8,128)} %bitcast.59), calls=%async_computation.1 | async-start | bytes 8388608 | tf_op jit(solution)/shard_map/all_to_all | solution.py:45
  150.1 25.9 %scatter_custom_fusion.3 = f32[8193]{0:T(1024)S(1)} fusion(s32[4096]{0:T(1024)S(1)} %bitcast.72, f32[4096]{0:T(1024)S(1)} %fusion.31, f32[]{:T(128)} %constant.86.clone.1), kind=kCustom, calls=%fused_computation.53 | custom fusion | flops 4096 | bytes 32776 | tf_op jit(solution)/shard_map/scatter-add | solution.py:63
  176.0 65.9 %all-to-all-done.1 = f32[16,256,256]{2,1,0:T(8,128)} async-done(((f32[16,256,256]{2,1,0:T(8,128)}), f32[16,256,256]{2,1,0:T(8,128)}, u32[]{:S(2)}, u32[]{:S(2)}) %all-to-all-start.1) | async-done | bytes 4194336 | tf_op jit(solution)/shard_map/all_to_all | solution.py:45
  242.0 29.9 %scatter_custom_fusion.2 = f32[8193,256]{1,0:T(8,128)} fusion(s32[4096]{0:T(1024)S(1)} %bitcast.73, f32[4096,256]{1,0:T(8,128)} %bitcast.11, f32[]{:T(128)} %constant.86.clone.1), kind=kCustom, calls=%fused_computation.8 | custom fusion | flops 1048576 | bytes 8390144 | tf_op jit(solution)/shard_map/scatter-add | solution.py:62
  271.9 3.4 slice-done
  275.3 1.2 copy-done
  276.5 5.2 %fusion.39 = (bf16[8,1024,256]{2,1,0:T(8,128)(2,1)}, f32[8,1024,256]{2,1,0:T(8,128)}) fusion(f32[8,1024]{1,0:T(8,128)S(1)} %add.166, f32[8,1024,256]{2,1,0:T(8,128)S(1)} %bitcast.57, bf16[8,1024,256]{2,1,0:T(8,128)(2,1)S(1)} %copy-done), kind=kLoop, calls=%fused_computation.101 | loop fusion | flops 8388608 | bytes 25198592 | tf_op jit(solution)/shard_map/convert_element_type | solution.py:83
  281.7 19.5 %gather_fusion = f32[4096,256]{1,0:T(8,128)} fusion(f32[8192,256]{1,0:T(8,128)} %bitcast.55, s32[4096]{0:T(1024)S(1)} %broadcast_clamp_fusion), kind=kCustom, calls=%fused_computation.1 | custom fusion | bytes 8404992 | tf_op jit(solution)/shard_map/jit(_take)/gather | solution.py:71
  301.2 5.7 %fusion.2 = bf16[16,256,256]{2,1,0:T(8,128)(2,1)} fusion(f32[16,256,256]{2,1,0:T(8,128)} %all-to-all-done.1, f32[16,256,256]{2,1,0:T(8,128)} %bitcast.58, pred[16,256]{1,0:T(8,128)(4,1)S(1)} %get-tuple-element.8, pred[16,256]{1,0:T(8,128)(4,1)S(1)} %get-tuple-element.7), kind=kLoop, calls=%fused_computation.11 | loop fusion | flops 4194304 | bytes 10493952 | tf_op jit(solution)/shard_map/jit(_where)/select_n | solution.py:74
  306.8 4.7 %all-to-all-start.2 = ((bf16[16,256,256]{2,1,0:T(8,128)(2,1)}), bf16[16,256,256]{2,1,0:T(8,128)(2,1)S(1)}, u32[]{:S(2)}, u32[]{:S(2)}) async-start(bf16[16,256,256]{2,1,0:T(8,128)(2,1)} %fusion.2), calls=%async_computation.2 | async-start | bytes 4194304 | tf_op jit(solution)/shard_map/all_to_all | solution.py:75
  311.6 47.4 %all-to-all-done.2 = bf16[16,256,256]{2,1,0:T(8,128)(2,1)S(1)} async-done(((bf16[16,256,256]{2,1,0:T(8,128)(2,1)}), bf16[16,256,256]{2,1,0:T(8,128)(2,1)S(1)}, u32[]{:S(2)}, u32[]{:S(2)}) %all-to-all-start.2) | async-done | bytes 2097184 | tf_op jit(solution)/shard_map/all_to_all | solution.py:75
  359.0 9.0 %gather_fusion.1 = bf16[2048,256]{1,0:T(8,128)(2,1)} fusion(bf16[4096,256]{1,0:T(8,128)(2,1)S(1)} %bitcast.56, s32[2048]{0:T(1024)S(1)} %broadcast_clamp_fusion.1), kind=kCustom, calls=%fused_computation.2 | custom fusion | bytes 2105344 | tf_op jit(solution)/shard_map/gather | solution.py:82
  (30 shorter events, 1.5 us)
Async XLA Ops:
  22.9 118.2 %all-to-all-start = ((s32[16,1,256]{2,1,0:T(1,128)}), s32[16,1,256]{2,1,0:T(1,128)S(1)}, u32[]{:S(2)}, u32[]{:S(2)}) async-start(s32[16,1,256]{2,1,0:T(1,128)} %bitcast.5), calls=%async_computation | async-start | bytes 32768 | tf_op jit(solution)/shard_map/all_to_all | solution.py:52
  29.5 91.3 %all-reduce.2.cloned.1.call-start = ((), (), s32[]{:S(2)}) async-start(), calls=%async_computation.3 | async-start | bytes 262144 | tf_op jit(solution)/shard_map/psum | solution.py:38
  121.8 19.3 %copy-start.1 = (f32[128,256]{1,0:T(8,128)}, f32[128,256]{1,0:T(8,128)S(1)}, u32[]{:S(2)}) copy-start(f32[128,256]{1,0:T(8,128)S(1)} %add_divide_fusion.1) | copy-start | bytes 393220
  141.1 8.4 %copy-start.2 = (s32[128]{0:T(128)S(1)}, s32[128]{0:T(128)}, u32[]{:S(2)}) copy-start(s32[128]{0:T(128)} %param.9) | copy-start | bytes 1540
  141.1 100.9 %all-to-all-start.1 = ((f32[16,256,256]{2,1,0:T(8,128)}), f32[16,256,256]{2,1,0:T(8,128)}, u32[]{:S(2)}, u32[]{:S(2)}) async-start(f32[16,256,256]{2,1,0:T(8,128)} %bitcast.59), calls=%async_computation.1 | async-start | bytes 8388608 | tf_op jit(solution)/shard_map/all_to_all | solution.py:45
  271.9 3.4 slice-start
  271.9 4.6 %copy-start = (bf16[8,1024,256]{2,1,0:T(8,128)(2,1)S(1)}, bf16[8,1024,256]{2,1,0:T(8,128)(2,1)}, u32[]{:S(2)}) copy-start(bf16[8,1024,256]{2,1,0:T(8,128)(2,1)} %param.11) | copy-start | bytes 12582916
  306.8 52.1 %all-to-all-start.2 = ((bf16[16,256,256]{2,1,0:T(8,128)(2,1)}), bf16[16,256,256]{2,1,0:T(8,128)(2,1)S(1)}, u32[]{:S(2)}, u32[]{:S(2)}) async-start(bf16[16,256,256]{2,1,0:T(8,128)(2,1)} %fusion.2), calls=%async_computation.2 | async-start | bytes 4194304 | tf_op jit(solution)/shard_map/all_to_all | solution.py:75
Sparse Core Ops, SparseCore 0:
  34.3 86.4 all-reduce.1
where the time goes:
time: 376 us; the launch traced here: 375 us
  waiting for transfers between devices  179 us (48%)
  other arithmetic  95.8 us (25%)
  local copies, waits for them, and re-layouts  42.2 us (11%)
  blocking collectives  21.7 us (6%)
  starting transfers between devices  19.7 us (5%)
  between operations  14.2 us (4%)
    all_to_all x1, waiting for transfers between devices, shards(): lax.all_to_all(row_buffer.reshape(owner_count, capacity, feature_width),...  65.9 us
    psum x1, waiting for transfers between devices, shards(): summed, counted = lax.psum((partial_value, tallies), 'owner')  65.7 us
    all_to_all x1, waiting for transfers between devices, shards(): lax.all_to_all(outgoing.reshape(owner_count, capacity, feature_width), 'o...  47.4 us
    scatter-add x1, other arithmetic, shards(): jax.ops.segment_sum(resid_in, segment, num_segments=dump_cell + 1)  29.9 us
    scatter-add x1, other arithmetic, shards(): jax.ops.segment_sum(live.astype(jnp.float32), segment, num_segments=dump_...  25.9 us
    psum x1, blocking collectives, shards(): summed, counted = lax.psum((partial_value, tallies), 'owner')  21.7 us
    gather x1, local copies, waits for them, and re-layouts, shards(): jnp.take(flat_refined, jnp.where(live, segment, 0), axis=0)  19.5 us
    scatter x1, other arithmetic, shards(): jnp.zeros((owner_count * capacity, feature_width), jnp.float32).at[position]  19.2 us
  transfers between devices with their start and end apart: 4, of which 3 were waited for; matrix products, arithmetic and copies ran while one was open for 13% of the time, Pallas kernels for 0%

commit v1 on v0

v1 whole, which is shorter than its diff:
```python
import functools

import jax
import jax.numpy as jnp
from jax import lax
from jax.experimental import pallas as pl
from jax.experimental.pallas import tpu as pltpu
from jax.sharding import PartitionSpec as P

prior_one = 16.0
prior_two = 1.0
tile = 256
digit_bits = 7
bf16 = jnp.bfloat16
f32 = jnp.float32
i32 = jnp.int32


def iota(shape, axis):
    return lax.broadcasted_iota(i32, shape, axis)


def shift_of(count):
    assert count & (count - 1) == 0
    return count.bit_length() - 1


def one_hot(hits):
    return jnp.where(hits, 1.0, 0.0).astype(bf16)


def dot(left, right):
    return jnp.dot(left, right, preferred_element_type=f32)


def exact_dot(left, right):
    return jnp.dot(left, right, preferred_element_type=f32, precision=lax.Precision.HIGHEST)


def column(row):
    size = row.shape[1]
    same = iota((size, size), 0) == iota((size, size), 1)
    return jnp.sum(jnp.where(same, row, 0), axis=1, keepdims=True)


def as_row(col):
    size = col.shape[0]
    same = iota((size, size), 0) == iota((size, size), 1)
    return jnp.sum(jnp.where(same, col, 0), axis=0, keepdims=True)


def kernel(
    owners,
    books,
    emb,
    code_one,
    code_two,
    slot_col,
    slot_row,
    cent_one,
    cent_two,
    new_one,
    new_two,
    resid,
    pos_row,
    pos_col,
    digits,
    send_codes,
    got_codes,
    cell_col,
    cell_row,
    packed,
    arrived,
    picked,
    shares,
    outgoing,
    returned,
    total,
    own_one,
    all_one,
    code_send,
    code_recv,
    row_send,
    row_recv,
    back_send,
    back_recv,
    one_send,
    one_recv,
):
    me = lax.axis_index("owner")
    rows, width = emb.shape
    parents = cent_one.shape[0]
    cells = cent_two.shape[0]
    words = cells // books
    slots = arrived.shape[0]
    cap = slots // owners
    word_shift = shift_of(words)
    book_shift = shift_of(books)

    def other(k):
        return lax.rem(me + k, owners)

    def block(index, size=cap):
        return pl.ds(pl.multiple_of(index * size, size), size)

    def codes_to(peer):
        return pltpu.make_async_remote_copy(
            src_ref=send_codes.at[peer],
            dst_ref=got_codes.at[me],
            send_sem=code_send.at[peer],
            recv_sem=code_recv.at[me],
            device_id={"owner": peer},
            device_id_type=pl.DeviceIdType.MESH,
        )

    def codes_from(peer):
        return pltpu.make_async_remote_copy(
            src_ref=send_codes.at[me],
            dst_ref=got_codes.at[peer],
            send_sem=code_send.at[me],
            recv_sem=code_recv.at[peer],
            device_id={"owner": peer},
            device_id_type=pl.DeviceIdType.MESH,
        )

    def block_copy(source, landing, send, recv, source_at, landing_at, peer, size=cap):
        return pltpu.make_async_remote_copy(
            src_ref=source.at[block(source_at, size)],
            dst_ref=landing.at[block(landing_at, size)],
            send_sem=send.at[source_at],
            recv_sem=recv.at[landing_at],
            device_id={"owner": peer},
            device_id_type=pl.DeviceIdType.MESH,
        )

    def rows_to(peer):
        return block_copy(packed, arrived, row_send, row_recv, peer, me, peer)

    def rows_from(peer):
        return block_copy(packed, arrived, row_send, row_recv, me, peer, peer)

    def back_to(peer):
        return block_copy(outgoing, returned, back_send, back_recv, peer, me, peer)

    def back_from(peer):
        return block_copy(outgoing, returned, back_send, back_recv, me, peer, peer)

    def one_copy(landing_at, sem_at, peer):
        return pltpu.make_async_remote_copy(
            src_ref=own_one.at[pl.ds(0, books)],
            dst_ref=all_one.at[block(landing_at, books)],
            send_sem=one_send.at[sem_at],
            recv_sem=one_recv.at[landing_at],
            device_id={"owner": peer},
            device_id_type=pl.DeviceIdType.MESH,
        )

    barrier = pltpu.get_barrier_semaphore()

    @pl.loop(1, owners)
    def _(k):
        pl.semaphore_signal(
            barrier, inc=1, device_id={"owner": other(k)}, device_id_type=pl.DeviceIdType.MESH
        )

    upto = one_hot(iota((tile, tile), 0) <= iota((tile, tile), 1))
    offset = jnp.zeros((owners, 1), f32)
    for part in range(rows // tile):
        span = slice(part * tile, (part + 1) * tile)
        codes = code_one[:, span]
        slot = jnp.sum(
            jnp.where(iota((parents, tile), 0) == codes, slot_col[...], 0), axis=0, keepdims=True
        )
        target = lax.shift_right_logical(slot, book_shift)
        hits = iota((owners, tile), 0) == target
        marks = jnp.where(hits, 1.0, 0.0)
        ranks = dot(marks.astype(bf16), upto) + offset
        offset = offset + jnp.sum(marks, axis=1, keepdims=True)
        place = jnp.sum(
            jnp.where(hits, iota((owners, tile), 0) * cap + ranks.astype(i32) - 1, 0),
            axis=0,
            keepdims=True,
        )
        cell = (slot - target * books) * words + code_two[:, span]
        pos_row[:, span] = place
        pos_col[span, :] = column(place)
        which = iota((16, tile), 0)
        high = lax.shift_right_logical(cell, digit_bits)
        low = cell & (2**digit_bits - 1)
        mixed = jnp.where(which == 0, high, jnp.where(which == 1, low, 1))
        digits[:, span] = mixed.astype(f32).astype(bf16)

    def select(peer):
        return one_hot(iota((cap, rows), 0) + peer * cap == pos_row[...])

    def make_codes(peer):
        sums = lax.dot_general(
            digits[...], select(peer), (((1,), (1,)), ((), ())), preferred_element_type=f32
        )
        code = sums[0:1] * 2.0**digit_bits + sums[1:2] + (sums[2:3] - 1.0)
        return jnp.broadcast_to(code.astype(i32), (8, cap))

    pl.semaphore_wait(barrier, owners - 1)

    @pl.loop(1, owners)
    def _(k):
        peer = other(k)
        send_codes[peer] = make_codes(peer)
        codes_to(peer).start()

    @pl.loop(1, owners)
    def _(k):
        peer = other(k)
        packed[block(peer), :] = dot(select(peer), emb[...]).astype(bf16)
        rows_to(peer).start()

    got_codes[me] = make_codes(me)
    arrived[block(me), :] = dot(select(me), emb[...]).astype(bf16)

    @pl.loop(1, owners)
    def _(k):
        codes_from(other(k)).wait_recv()

    @pl.loop(0, owners)
    def _(s):
        cell_col[block(s), :] = column(got_codes[s][0:1, :])

    @pl.loop(0, slots // tile)
    def _(t):
        cell_row[:, block(t, tile)] = as_row(cell_col[block(t, tile), :])

    span = min(cells, 2048)

    @pl.loop(0, slots // tile)
    def _(t):
        mine = cell_col[block(t, tile), :]
        count = jnp.sum(jnp.where(mine == cell_row[...], 1.0, 0.0), axis=1, keepdims=True)
        shares[block(t, tile), :] = count + prior_two
        found = jnp.zeros((tile, width), f32)
        for at in range(0, cells, span):
            chosen = one_hot(mine - at == iota((tile, span), 1))
            found = found + dot(chosen, cent_two[at : at + span, :])
        picked[block(t, tile), :] = found.astype(bf16)

    @pl.loop(1, owners)
    def _(k):
        rows_from(other(k)).wait_recv()

    marks = jnp.where(
        iota((16, slots), 0) == lax.shift_right_arithmetic(cell_row[...], word_shift), 1.0, 0.0
    )
    sums = dot(marks.astype(bf16), arrived[...])
    tally = jnp.sum(marks, axis=1, keepdims=True)
    held = iota((16, parents), 0)
    chosen = jnp.where((slot_row[...] == held + me * books) & (held < books), 1.0, 0.0)
    own_one[...] = (sums + prior_one * exact_dot(chosen, cent_one[...])) / (tally + prior_one)

    def second(peer):
        mine = cell_col[block(peer), :]
        sums = dot(one_hot(mine == cell_row[...]), arrived[...])
        sums = sums + picked[block(peer), :].astype(f32)
        book = lax.shift_right_arithmetic(mine, word_shift)
        for b in range(books):
            sums = sums + jnp.where(book == b, own_one[b : b + 1, :], 0.0)
        value = arrived[block(peer), :].astype(f32) - sums / shares[block(peer), :]
        return value.astype(bf16)

    @pl.loop(1, owners)
    def _(k):
        peer = other(k)
        outgoing[block(peer), :] = second(peer)
        back_to(peer).start()

    @pl.loop(1, owners)
    def _(k):
        one_copy(me, other(k), other(k)).start()

    all_one[block(me, books), :] = own_one[0:books, :]
    returned[block(me), :] = second(me)

    high = min(words, 512)

    @pl.loop(0, cells // high)
    def _(t):
        base = own_one[pl.ds(t // (words // high), 1), :]
        sums = jnp.zeros((high, width), f32)
        count = jnp.zeros((high, 1), f32)
        half = min(slots, 2048)
        for at in range(0, slots, half):
            marks = jnp.where(
                iota((high, half), 0) + t * high == cell_row[:, at : at + half], 1.0, 0.0
            )
            count = count + jnp.sum(marks, axis=1, keepdims=True)
            sums = sums + dot(marks.astype(bf16), arrived[at : at + half, :])
        old = cent_two[block(t, high), :].astype(f32)
        fresh = (sums - count * base + prior_two * old) / (count + prior_two)
        new_two[block(t, high), :] = fresh.astype(bf16)

    def put_back(peer):
        chosen = one_hot(pos_col[...] - peer * cap == iota((rows, cap), 1))
        return dot(chosen, returned[block(peer), :])

    total[...] = put_back(me)

    @pl.loop(1, owners)
    def _(k):
        peer = other(owners - k)
        back_from(peer).wait_recv()
        total[...] += put_back(peer)

    resid[...] = total[...].astype(bf16)

    @pl.loop(1, owners)
    def _(k):
        peer = other(k)
        one_copy(peer, me, peer).wait_recv()

    new_one[...] = exact_dot(
        jnp.where(slot_col[...] == iota((parents, parents), 1), 1.0, 0.0), all_one[...]
    )

    @pl.loop(1, owners)
    def _(k):
        peer = other(k)
        codes_to(peer).wait_send()
        rows_to(peer).wait_send()
        back_to(peer).wait_send()
        one_copy(me, peer, peer).wait_send()


def shards(embeddings, code_one, code_two, parent_slot, centers_one, centers_two):
    rows, width = embeddings.shape
    owners = lax.axis_size("owner")
    parents = centers_one.shape[0]
    books, words, _ = centers_two.shape
    cells = books * words
    cap = 2 * rows // owners
    slots = owners * cap
    vmem = pl.BlockSpec(memory_space=pltpu.VMEM)
    new_one, new_two, resid = pl.pallas_call(
        functools.partial(kernel, owners, books),
        out_shape=(
            jax.ShapeDtypeStruct((parents, width), f32),
            jax.ShapeDtypeStruct((cells, width), bf16),
            jax.ShapeDtypeStruct((rows, width), bf16),
        ),
        in_specs=[vmem] * 7,
        out_specs=(vmem,) * 3,
        scratch_shapes=[
            pltpu.VMEM((1, rows), i32),
            pltpu.VMEM((rows, 1), i32),
            pltpu.VMEM((16, rows), bf16),
            pltpu.VMEM((owners, 8, cap), i32),
            pltpu.VMEM((owners, 8, cap), i32),
            pltpu.VMEM((slots, 1), i32),
            pltpu.VMEM((1, slots), i32),
            pltpu.VMEM((slots, width), bf16),
            pltpu.VMEM((slots, width), bf16),
            pltpu.VMEM((slots, width), bf16),
            pltpu.VMEM((slots, 1), f32),
            pltpu.VMEM((slots, width), bf16),
            pltpu.VMEM((slots, width), bf16),
            pltpu.VMEM((rows, width), f32),
            pltpu.VMEM((16, width), f32),
            pltpu.VMEM((owners * books, width), f32),
        ]
        + [pltpu.SemaphoreType.DMA((owners,))] * 8,
        compiler_params=pltpu.CompilerParams(
            collective_id=0, has_side_effects=True, vmem_limit_bytes=56 * 2**20
        ),
        name="refine",
    )(
        embeddings,
        code_one.reshape(1, rows),
        code_two.reshape(1, rows),
        parent_slot.reshape(parents, 1),
        parent_slot.reshape(1, parents),
        centers_one,
        centers_two.reshape(cells, width),
    )
    return new_one, new_two.reshape(books, words, width), resid


def solution(mesh):
    placed = (
        P(("groups", "owner"), None),
        P(("groups", "owner")),
        P(("groups", "owner")),
        P("groups"),
        P("groups", None),
        P(("groups", "owner"), None, None),
    )
    return jax.shard_map(
        shards,
        mesh=mesh,
        in_specs=placed,
        out_specs=(
            P("groups", None),
            P(("groups", "owner"), None, None),
            P(("groups", "owner"), None),
        ),
        check_vma=False,
    )
```

time: 376 us -> 129 us (0.34)
  waiting for transfers between devices: 179 us -> 0 us
  Pallas kernels: 0 us -> 119 us
  other arithmetic: 95.8 us -> 0 us
  local copies, waits for them, and re-layouts: 42.2 us -> 8.49 us
  blocking collectives: 21.7 us -> 0 us
  starting transfers between devices: 19.7 us -> 0 us
  between operations: 14.2 us -> 0.64 us
    pallas_call x0 -> x1, Pallas kernels: none -> 119 us  [shards(): pl.pallas_call(functools.partial(kernel, owners, books), out_shape=(jax.S...]
    all_to_all x3 -> x0, waiting for transfers between devices: 113 us -> none  [the longest x1 65.9 us: shards(): lax.all_to_all(row_buffer.reshape(owner_count, capacity, feature_width),...]
    psum x1 -> x0, waiting for transfers between devices: 65.7 us -> none  [shards(): summed, counted = lax.psum((partial_value, tallies), 'owner')]
    scatter-add x2 -> x0, other arithmetic: 55.8 us -> none  [the longest x1 29.9 us: shards(): jax.ops.segment_sum(resid_in, segment, num_segments=dump_cell + 1)]
    gather x2 -> x0, local copies, waits for them, and re-layouts: 28.5 us -> none  [the longest x1 19.5 us: shards(): jnp.take(flat_refined, jnp.where(live, segment, 0), axis=0)]
    psum x1 -> x0, blocking collectives: 21.7 us -> none  [shards(): summed, counted = lax.psum((partial_value, tallies), 'owner')]
    all_to_all x3 -> x0, starting transfers between devices: 19.7 us -> none  [the longest x1 8.4 us: shards(): lax.all_to_all(row_buffer.reshape(owner_count, capacity, feature_width),...]
    scatter x1 -> x0, other arithmetic: 19.2 us -> none  [shards(): jnp.zeros((owner_count * capacity, feature_width), jnp.float32).at[position]]
  transfers between devices with their start and end apart: 4 -> 0, of which waited for: 3 -> 0; matrix products, arithmetic and copies ran while one was open for 13% -> 0% of each run, Pallas kernels for 0% -> 0%
where the time goes in v1:
time: 129 us; the launch traced here: 128 us
  Pallas kernels  119 us (92%)
  local copies, waits for them, and re-layouts  8.49 us (7%)
    pallas_call x1, Pallas kernels, shards(): pl.pallas_call(functools.partial(kernel, owners, books), out_shape=(jax.S...  119 us
    unnamed x5, local copies, waits for them, and re-layouts  7.1 us

profile of v1, /device:TPU:13, one launch (start us, length us, event | category | flops | bytes accessed | tf_op | source)
XLA Modules:
  0.0 128.4 jit_solution(17579821834991816637)
XLA Ops:
  0.6 1.4 %copy.9.slot_col = s32[128,1]{1,0:T(8,128)} copy(s32[128,1]{0,1:T(1,128)} %bitcast.10) | data formatting | bytes 1024 | tf_op jit(solution)/shard_map/reshape | solution.py:376
  2.0 119.3 %refine.1 = (f32[128,256]{1,0:T(8,128)}, bf16[8192,256]{1,0:T(8,128)(2,1)}, bf16[2048,256]{1,0:T(8,128)(2,1)}) custom-call(bf16[2048,256]{1,0:T(8,128)(2,1)} %emb.1, s32[1,2048]{1,0:T(1,128)} %bitcast.8, s32[1,2048]{1,0:T(1,128)} %bitcast.9, s32[128,1]{1,0:T(8,128)} %copy.9.slot_col, s32[1,128]{1,0:T(1,128)} %bitcast.11, f32[128,256]{1,0:T(8,128)} %cent_one.1, ...), custom_call_target="tpu_custom_call" | custom-call | tf_op jit(solution)/shard_map/refine/pallas_call | solution.py:340
  121.3 1.6 %copy.13 = f32[128,256]{1,0:T(8,128)} copy(f32[128,256]{1,0:T(8,128)} %get-tuple-element.12) | data formatting | bytes 262144
  122.9 0.0 copy-start
  122.9 4.6 %copy.14 = bf16[8,1024,256]{2,1,0:T(8,128)(2,1)} copy(bf16[8,1024,256]{2,1,0:T(8,128)(2,1)} %bitcast.7) | data formatting | bytes 8388608
  127.4 0.0 copy-done
  127.4 1.0 copy.15
Async XLA Ops:
  122.9 4.6 %copy-start = (bf16[2048,256]{1,0:T(8,128)(2,1)S(1)}, bf16[2048,256]{1,0:T(8,128)(2,1)}, u32[]{:S(2)}) copy-start(bf16[2048,256]{1,0:T(8,128)(2,1)} %get-tuple-element.14) | copy-start | bytes 3145732

commit v2 on v1

--- a/solution.py
+++ b/solution.py
@@ -11,6 +11,7 @@
 prior_two = 1.0
 tile = 256
 digit_bits = 7
+pieces = 8
 bf16 = jnp.bfloat16
 f32 = jnp.float32
 i32 = jnp.int32
@@ -55,13 +56,15 @@
     emb,
     code_one,
     code_two,
-    slot_col,
     slot_row,
     cent_one,
     cent_two,
     new_one,
     new_two,
     resid,
+    slot_col,
+    old_two,
+    fresh_two,
     pos_row,
     pos_col,
     digits,
@@ -86,6 +89,9 @@
     back_recv,
     one_send,
     one_recv,
+    load_sem,
+    save_sem,
+    ready,
 ):
     me = lax.axis_index("owner")
     rows, width = emb.shape
@@ -98,7 +104,7 @@
     book_shift = shift_of(books)
 
     def other(k):
-        return lax.rem(me + k, owners)
+        return lax.rem(me + owners // 2 + (1 - k % 2 * 2) * (k // 2) + owners, owners)
 
     def block(index, size=cap):
         return pl.ds(pl.multiple_of(index * size, size), size)
@@ -155,6 +161,8 @@
             device_id_type=pl.DeviceIdType.MESH,
         )
 
+    load_two = pltpu.make_async_copy(cent_two, old_two, load_sem)
+    load_two.start()
     barrier = pltpu.get_barrier_semaphore()
 
     @pl.loop(1, owners)
@@ -162,6 +170,10 @@
         pl.semaphore_signal(
             barrier, inc=1, device_id={"owner": other(k)}, device_id_type=pl.DeviceIdType.MESH
         )
+
+    piece = min(parents, tile)
+    for at in range(0, parents, piece):
+        slot_col[at : at + piece, :] = column(slot_row[:, at : at + piece])
 
     upto = one_hot(iota((tile, tile), 0) <= iota((tile, tile), 1))
     offset = jnp.zeros((owners, 1), f32)
@@ -230,6 +242,7 @@
         cell_row[:, block(t, tile)] = as_row(cell_col[block(t, tile), :])
 
     span = min(cells, 2048)
+    load_two.wait()
 
     @pl.loop(0, slots // tile)
     def _(t):
@@ -239,12 +252,18 @@
         found = jnp.zeros((tile, width), f32)
         for at in range(0, cells, span):
             chosen = one_hot(mine - at == iota((tile, span), 1))
-            found = found + dot(chosen, cent_two[at : at + span, :])
+            found = found + dot(chosen, old_two[at : at + span, :])
         picked[block(t, tile), :] = found.astype(bf16)
 
     @pl.loop(1, owners)
     def _(k):
         rows_from(other(k)).wait_recv()
+
+    @pl.loop(1, owners)
+    def _(k):
+        pl.semaphore_signal(
+            ready, inc=1, device_id={"owner": other(k)}, device_id_type=pl.DeviceIdType.MESH
+        )
 
     marks = jnp.where(
         iota((16, slots), 0) == lax.shift_right_arithmetic(cell_row[...], word_shift), 1.0, 0.0
@@ -254,6 +273,12 @@
     held = iota((16, parents), 0)
     chosen = jnp.where((slot_row[...] == held + me * books) & (held < books), 1.0, 0.0)
     own_one[...] = (sums + prior_one * exact_dot(chosen, cent_one[...])) / (tally + prior_one)
+
+    @pl.loop(1, owners)
+    def _(k):
+        one_copy(me, other(k), other(k)).start()
+
+    all_one[block(me, books), :] = own_one[0:books, :]
 
     def second(peer):
         mine = cell_col[block(peer), :]
@@ -265,20 +290,22 @@
         value = arrived[block(peer), :].astype(f32) - sums / shares[block(peer), :]
         return value.astype(bf16)
 
+    returned[block(me), :] = second(me)
+    pl.semaphore_wait(ready, owners - 1)
+
     @pl.loop(1, owners)
     def _(k):
         peer = other(k)
         outgoing[block(peer), :] = second(peer)
         back_to(peer).start()
 
-    @pl.loop(1, owners)
-    def _(k):
-        one_copy(me, other(k), other(k)).start()
-
-    all_one[block(me, books), :] = own_one[0:books, :]
-    returned[block(me), :] = second(me)
 
     high = min(words, 512)
+
+    def save(t):
+        return pltpu.make_async_copy(
+            fresh_two.at[block(t, high)], new_two.at[block(t, high)], save_sem.at[t]
+        )
 
     @pl.loop(0, cells // high)
     def _(t):
@@ -292,9 +319,10 @@
             )
             count = count + jnp.sum(marks, axis=1, keepdims=True)
             sums = sums + dot(marks.astype(bf16), arrived[at : at + half, :])
-        old = cent_two[block(t, high), :].astype(f32)
+        old = old_two[block(t, high), :].astype(f32)
         fresh = (sums - count * base + prior_two * old) / (count + prior_two)
-        new_two[block(t, high), :] = fresh.astype(bf16)
+        fresh_two[block(t, high), :] = fresh.astype(bf16)
+        save(t).start()
 
     def put_back(peer):
         chosen = one_hot(pos_col[...] - peer * cap == iota((rows, cap), 1))
@@ -304,7 +332,7 @@
 
     @pl.loop(1, owners)
     def _(k):
-        peer = other(owners - k)
+        peer = other(k)
         back_from(peer).wait_recv()
         total[...] += put_back(peer)
 
@@ -326,6 +354,31 @@
         rows_to(peer).wait_send()
         back_to(peer).wait_send()
         one_copy(me, peer, peer).wait_send()
+
+    @pl.loop(0, cells // high)
+    def _(t):
+        save(t).wait()
+
+
+def hand_on(one_in, two_in, resid_in, one_out, two_out, resid_out, one, two, resid, loads, saves):
+    part = two_in.shape[0] // pieces
+    moves = [(resid_in, resid, resid_out), (one_in, one, one_out)]
+    for i in range(pieces):
+        span = pl.ds(i * part, part)
+        moves.append((two_in.at[span], two.at[span], two_out.at[span]))
+    into = [
+        pltpu.make_async_copy(move[0], move[1], loads.at[i]) for i, move in enumerate(moves)
+    ]
+    out_of = [
+        pltpu.make_async_copy(move[1], move[2], saves.at[i]) for i, move in enumerate(moves)
+    ]
+    for copy in into:
+        copy.start()
+    for first, then in zip(into, out_of):
+        first.wait()
+        then.start()
+    for copy in out_of:
+        copy.wait()
 
 
 def shards(embeddings, code_one, code_two, parent_slot, centers_one, centers_two):
@@ -344,9 +397,12 @@
             jax.ShapeDtypeStruct((cells, width), bf16),
             jax.ShapeDtypeStruct((rows, width), bf16),
         ),
-        in_specs=[vmem] * 7,
-        out_specs=(vmem,) * 3,
+        in_specs=[vmem] * 5 + [pl.BlockSpec(memory_space=pl.ANY)],
+        out_specs=(vmem, pl.BlockSpec(memory_space=pl.ANY), vmem),
         scratch_shapes=[
+            pltpu.VMEM((parents, 1), i32),
+            pltpu.VMEM((cells, width), bf16),
+            pltpu.VMEM((cells, width), bf16),
             pltpu.VMEM((1, rows), i32),
             pltpu.VMEM((rows, 1), i32),
             pltpu.VMEM((16, rows), bf16),
@@ -364,7 +420,9 @@
             pltpu.VMEM((16, width), f32),
             pltpu.VMEM((owners * books, width), f32),
         ]
-        + [pltpu.SemaphoreType.DMA((owners,))] * 8,
+        + [pltpu.SemaphoreType.DMA((owners,))] * 8
+        + [pltpu.SemaphoreType.DMA, pltpu.SemaphoreType.DMA((cells // min(words, 512),))]
+        + [pltpu.SemaphoreType.REGULAR],
         compiler_params=pltpu.CompilerParams(
             collective_id=0, has_side_effects=True, vmem_limit_bytes=56 * 2**20
         ),
@@ -373,11 +431,22 @@
         embeddings,
         code_one.reshape(1, rows),
         code_two.reshape(1, rows),
-        parent_slot.reshape(parents, 1),
         parent_slot.reshape(1, parents),
         centers_one,
         centers_two.reshape(cells, width),
     )
+    hbm = pl.BlockSpec(memory_space=pl.ANY)
+    results = (new_one, new_two, resid)
+    new_one, new_two, resid = pl.pallas_call(
+        hand_on,
+        out_shape=tuple(jax.ShapeDtypeStruct(x.shape, x.dtype) for x in results),
+        in_specs=[hbm] * 3,
+        out_specs=(hbm,) * 3,
+        scratch_shapes=[pltpu.VMEM(x.shape, x.dtype) for x in results]
+        + [pltpu.SemaphoreType.DMA((2 + pieces,))] * 2,
+        compiler_params=pltpu.CompilerParams(vmem_limit_bytes=56 * 2**20),
+        name="hand_on",
+    )(*results)
     return new_one, new_two.reshape(books, words, width), resid
 
 

time: 129 us -> 125 us (0.969)
  local copies, waits for them, and re-layouts: 8.49 us -> 0 us
  Pallas kernels: 119 us -> 123 us
    unnamed x5 -> x0, local copies, waits for them, and re-layouts: 7.1 us -> none
    pallas_call x0 -> x1, Pallas kernels: none -> 4.39 us  [shards(): pl.pallas_call(hand_on, out_shape=tuple((jax.ShapeDtypeStruct(x.shape, x....]
    reshape x1 -> x0, local copies, waits for them, and re-layouts: 1.39 us -> none  [shards(): parent_slot.reshape(parents, 1)]
where the time goes in v2:
time: 125 us; the launch traced here: 123 us
  Pallas kernels  123 us (98%)
    pallas_call x1, Pallas kernels, shards(): pl.pallas_call(functools.partial(kernel, owners, books), out_shape=(jax.S...  118 us
    pallas_call x1, Pallas kernels, shards(): pl.pallas_call(hand_on, out_shape=tuple((jax.ShapeDtypeStruct(x.shape, x....  4.39 us

profile of v2, /device:TPU:13, one launch (start us, length us, event | category | flops | bytes accessed | tf_op | source)
XLA Modules:
  0.0 123.3 jit_solution(5612615015316005865)
XLA Ops:
  0.6 118.2 %refine.1 = (f32[128,256]{1,0:T(8,128)}, bf16[8192,256]{1,0:T(8,128)(2,1)}, bf16[2048,256]{1,0:T(8,128)(2,1)}) custom-call(bf16[2048,256]{1,0:T(8,128)(2,1)} %emb.1, s32[1,2048]{1,0:T(1,128)} %bitcast.6, s32[1,2048]{1,0:T(1,128)} %bitcast.7, s32[1,128]{1,0:T(1,128)} %bitcast.8, f32[128,256]{1,0:T(8,128)} %cent_one.1, bf16[8192,256]{1,0:T(8,128)(2,1)} %bitcast.5), custom_call_target="tpu_custom_call" | custom-call | tf_op jit(solution)/shard_map/refine/pallas_call | solution.py:393
  118.9 4.4 %hand_on.1 = (f32[128,256]{1,0:T(8,128)}, bf16[8192,256]{1,0:T(8,128)(2,1)}, bf16[2048,256]{1,0:T(8,128)(2,1)}) custom-call(f32[128,256]{1,0:T(8,128)} %get-tuple-element.9.one_in, bf16[8192,256]{1,0:T(8,128)(2,1)} %get-tuple-element.10.two_in, bf16[2048,256]{1,0:T(8,128)(2,1)} %get-tuple-element.11.resid_in), custom_call_target="tpu_custom_call" | custom-call | tf_op jit(solution)/shard_map/hand_on/pallas_call | solution.py:440
